TPU v7x, 256 devices: a whole 4x4x8 slice. The times are simulated.
256 devices in a mesh: leaf: 128 (over z, x, y), sub: 2 (over core).
Axes of the slice: x: 4, y: 4, z: 8, core: 2. Of those that a mesh axis runs over, the one named last changes fastest.
Arguments:
- probes: float32 [64, 262144], P(None, ('leaf', 'sub')), may hold values from -600 to 600
- points: float32 [3, 262144], P(None, ('leaf', 'sub')), may hold values from -22 to 22
- leaf_order: int32 [262144], P(('leaf', 'sub')), may hold values from 0 to 1023, as said below
- near_list: int32 [512, 4], P(('leaf', 'sub')), may hold values from 0 to 511, as said below
- far_leaf_list: int32 [512, 2], P(('leaf', 'sub')), may hold values from 0 to 511, as said below
- far_chip_list: int32 [128, 8], P('leaf'), may hold values from -1 to 127, as said below
- leaf_basis: float32 [512, 512, 256], P(('leaf', 'sub')), may hold values from -0.25 to 0.25
- transfer: float32 [512, 256, 256], P(('leaf', 'sub')), may hold values from -0.1875 to 0.1875
- far_leaf_blocks: float32 [1024, 256, 256], P(('leaf', 'sub')), may hold values from -0.25 to 0.25
- far_chip_blocks: float32 [1024, 256, 256], P('leaf'), may hold values from -0.125 to 0.125
Outputs:
- result: float32 [64, 262144], P(None, ('leaf', 'sub'))
Inputs may be any that keep to these rules, and one draw needn't show every extreme that they name: `leaf_order`: each device's block of 1024 consecutive entries is a permutation of 0 to 1023. `near_list`: row l lists 4 distinct leaves, l among them, all held by the devices l // 2 - 1 to l // 2 + 1 of the joined axis leaf+sub, counted around the cycle. `far_leaf_list`: row l lists the 2 leaves of those same three devices that row l of near_list leaves out. `far_chip_list`: row k lists distinct chip clusters at cycle distance 2 to 5 from k, one to 8 of them, the used entries first and -1 in the rest; some row uses all 8.
All inputs are finite; a program needn't handle non-finite values.
Results may differ from a plain program's by a relative error of at most 0.0003.
Values sent between devices are 32-bit elements; how exact they have to be, the bound alone decides.
A program may use at most 64 MiB of HBM per device.

v0:
```python
import math

import jax
import jax.numpy as jnp
from jax import lax
from jax.experimental import pallas as pl
from jax.experimental.pallas import tpu as pltpu
from jax.sharding import PartitionSpec as P

F32 = jnp.float32
BF16 = jnp.bfloat16
MESH = pl.DeviceIdType.MESH

COLS = 64
LEAF = 512
RANK = 256
CHIPS = 128
LEAVES = 512
DEVICES = 256
POINTS = 262144
NY = 4
NX = 4
NZ = 8
DISTANCES = (2, 3, 4, 5)
EXPONENT = -0.5 / (0.15 * 0.15) * math.log2(math.e)
EPSILON = 1e-6
NN = (((1,), (0,)), ((), ()))
NT = (((1,), (1,)), ((), ()))


def parts_of(x):
    high = x.astype(BF16)
    return high, (x - high.astype(F32)).astype(BF16)


def stacked(x):
    return jnp.concatenate(parts_of(x), axis=0)


def product(both, w_high, w_low, dims=NN):
    rows = both.shape[0] // 2
    main = lax.dot_general(both, w_high, dims, preferred_element_type=F32)
    rest = lax.dot_general(both[:rows], w_low, dims, preferred_element_type=F32)
    return main[:rows] + main[rows:] + rest


def kernel(
    near_ref, far_ref, chip_ref,
    probes_hbm, points_hbm, order_hbm, basis_hbm, transfer_hbm, leafblk_hbm, chipblk_hbm,
    out_ref,
    probes, points, order, basis, transfer, leafblk, chipblk,
    perm, basis_h, basis_l, trans_h, trans_l, leaf_h, leaf_l, chip_h, chip_l,
    kern_h, kern_l, turned, pwin, vwin0, vwin1, cwin0, cwin1,
    gown, grecv, gsum, gchip, hown, hrecv, near, sqown, sqrecv,
    local_sem, send_sem, recv_sem,
):
    vwin = (vwin0, vwin1)
    cwin = (cwin0, cwin1)
    leaf = lax.axis_index("leaf")
    sub = lax.axis_index("sub")
    other = 1 - sub
    dev = 2 * leaf + sub
    sign = 2 * sub - 1
    y = leaf % NY
    x = (leaf // NY) % NX
    z = leaf // (NY * NX)
    nxt = ((dev + 1) % DEVICES) // 2
    prv = ((dev + DEVICES - 1) % DEVICES) // 2

    loads = []
    for n, (src, dst) in enumerate((
        (order_hbm, order), (points_hbm, points), (probes_hbm, probes), (basis_hbm, basis),
        (transfer_hbm, transfer), (chipblk_hbm, chipblk), (leafblk_hbm, leafblk),
    )):
        copy = pltpu.make_async_copy(src, dst, local_sem.at[n])
        copy.start()
        loads.append(copy)
    ld_order, ld_points, ld_probes, ld_basis, ld_transfer, ld_chip, ld_leaf = loads

    def chip_of(dz, dx, dy):
        return (((z + dz) % NZ) * NX + (x + dx) % NX) * NY + (y + dy) % NY

    rounds = (
        [(chip_of(0, 0, dy), (sub + ds) % 2) for dy in range(NY) for ds in range(2) if dy + ds > 0],
        [(chip_of(0, dx, 0), sub) for dx in range(1, NX)],
        [(chip_of(dz, 0, 0), sub) for dz in range(1, NZ)],
    )

    barrier = pltpu.get_barrier_semaphore()
    senders = [(nxt, other), (prv, other)]
    senders += [((leaf - sign * d + CHIPS) % CHIPS, sub) for d in DISTANCES]
    senders += [who for group in rounds for who in group]
    for who in senders:
        pl.semaphore_signal(barrier, inc=1, device_id=who, device_id_type=MESH)

    ld_order.wait()
    row = lax.broadcasted_iota(jnp.int32, (1024, 128), 0)
    for r in range(8):
        perm[:, r * 128:(r + 1) * 128] = (row == order[r:r + 1, :]).astype(F32).astype(BF16)
    ld_points.wait()
    pts = points[...]
    p_1 = pts.astype(BF16).astype(F32)
    p_2 = (pts - p_1).astype(BF16).astype(F32)
    p_3 = (pts - p_1) - p_2
    zero5 = jnp.zeros((5, 1024), F32)
    zero8 = jnp.zeros((8, 1024), F32)
    p_all = jnp.concatenate([p_1, zero5, p_2, zero5, p_3, zero5, zero8], axis=0).astype(BF16)
    p_sorted = lax.dot_general(p_all, perm[...], NN, preferred_element_type=F32)
    p_sorted = (p_sorted[0:8] + p_sorted[8:16]) + p_sorted[16:24]
    for l in range(2):
        pwin[2 + l] = p_sorted[:, l * LEAF:(l + 1) * LEAF]

    pl.semaphore_wait(barrier, len(senders))

    sent = []
    count = [0]

    def send(src, dst, who):
        n = count[0]
        count[0] += 1
        copy = pltpu.make_async_remote_copy(
            src_ref=src, dst_ref=dst, send_sem=send_sem.at[n], recv_sem=recv_sem.at[n],
            device_id=who, device_id_type=MESH,
        )
        copy.start()
        sent.append(copy)
        return copy

    def both_ways(ref):
        return (
            send(ref.at[pl.ds(2, 2)], ref.at[pl.ds(0, 2)], (nxt, other)),
            send(ref.at[pl.ds(2, 2)], ref.at[pl.ds(4, 2)], (prv, other)),
        )

    points_in = both_ways(pwin)

    ld_probes.wait()
    v_sorted = lax.dot_general(stacked(probes[...]), perm[...], NN, preferred_element_type=F32)
    v_sorted = v_sorted[:COLS] + v_sorted[COLS:]
    for l in range(2):
        vwin[0][2 + l] = v_sorted[:, l * LEAF:(l + 1) * LEAF]

    first_leaf = 2 * (dev - 1)

    def place(listed):
        return jnp.clip(lax.rem(listed - first_leaf + 2 * LEAVES, LEAVES), 0, 5)

    def near_place(l, j):
        listed = near_ref[l, j]
        return place(jnp.where(listed == 2 * dev + l, near_ref[l, 3], listed))

    def split_into(src, high, low, at, rows):
        def step(i, _):
            part = pl.ds(pl.multiple_of(i * 64, 64), 64)
            a, b = parts_of(src[at, part, :])
            high[at, part, :] = a
            low[at, part, :] = b
            return 0
        lax.fori_loop(0, rows // 64, step, 0)

    def tile(l, j, source):
        target = pwin[2 + l]
        tx, ty, tz = target[0:1], target[1:2], target[2:3]

        def step(i, _):
            part = pl.ds(pl.multiple_of(i * 32, 32), 32)
            s = turned[source, part, :]
            dx = s[:, 0:1] - tx
            dy = s[:, 1:2] - ty
            dz = s[:, 2:3] - tz
            a, b = parts_of(jnp.exp2((dx * dx + dy * dy + dz * dz) * EXPONENT))
            kern_h[4 * l + j, part, :] = a
            kern_l[4 * l + j, part, :] = b
            return 0
        lax.fori_loop(0, LEAF // 32, step, 0)

    def turn(w):
        whole = jnp.concatenate([pwin[w], jnp.zeros((120, LEAF), F32)], axis=0)
        turned[w] = jnp.transpose(whole)

    def near_term(p, l, j, w):
        return product(stacked(vwin[p][w]), kern_h[4 * l + j], kern_l[4 * l + j])

    def sum_round(r, copies):
        base = (0, 7, 10)[r]
        for i, copy in enumerate(copies):
            copy.wait_recv()
        total = sqown[r]
        for i in range(len(copies)):
            total = total + sqrecv[base + i]
        return total

    def start_round(r, total):
        base = (0, 7, 10)[r]
        sqown[r] = total
        return [send(sqown.at[r], sqrecv.at[base + i], who) for i, who in enumerate(rounds[r])]

    squares = None
    for p in range(2):
        if p == 0:
            ld_basis.wait()
            for l in range(2):
                split_into(basis, basis_h, basis_l, l, LEAF)
        up = []
        for l in range(2):
            c = product(stacked(vwin[p][2 + l]), basis_h[l], basis_l[l])
            cwin[p][2 + l] = c
            up.append(c)
        if p == 0:
            ld_transfer.wait()
            for l in range(2):
                split_into(transfer, trans_h, trans_l, l, RANK)
        gown[p] = sum(product(stacked(up[l]), trans_h[l], trans_l[l]) for l in range(2))
        g_in = send(gown.at[p], grecv.at[p], (leaf, other))
        values_in = None
        if p == 0:
            values_in = both_ways(vwin[p])
            for l in range(2):
                turn(2 + l)
        if p == 0:
            for l in range(2):
                tile(l, 3, 2 + l)
        g_in.wait_recv()
        gsum[p] = gown[p] + grecv[p]
        chips_in = [
            send(gsum.at[p], gchip.at[p, i], ((leaf + sign * d + CHIPS) % CHIPS, sub))
            for i, d in enumerate(DISTANCES)
        ]
        if values_in is None:
            values_in = both_ways(vwin[p])
        coeff_in = both_ways(cwin[p])
        if p == 1:
            v = jnp.concatenate([vwin[p][2], vwin[p][3]], axis=1)
            v = v * v
            total = lax.dot_general(
                jnp.ones((8, 1024), F32), jnp.concatenate([v, v], axis=0), NT,
                precision=lax.Precision.HIGHEST, preferred_element_type=F32,
            )
            squares = start_round(0, total)
        for l in range(2):
            near[l] = near_term(p, l, 3, 2 + l)
        if p == 0:
            ld_chip.wait()
            for i, d in enumerate(DISTANCES):
                want = jnp.where(sub == 0, d, CHIPS - d)
                slot = jnp.int32(0)
                found = jnp.int32(0)
                for j in range(8):
                    listed = chip_ref[0, j]
                    hit = jnp.where(
                        (listed >= 0) & (lax.rem(listed - leaf + CHIPS, CHIPS) == want), 1, 0
                    )
                    slot = slot + j * hit
                    found = found + hit
                slot = jnp.clip(slot, 0, 7)
                weight = found.astype(F32)

                def step(k, _, i=i, slot=slot, weight=weight):
                    part = pl.ds(pl.multiple_of(k * 64, 64), 64)
                    a, b = parts_of(chipblk[slot, part, :] * weight)
                    chip_h[i, part, :] = a
                    chip_l[i, part, :] = b
                    return 0
                lax.fori_loop(0, RANK // 64, step, 0)
            ld_leaf.wait()
            for n in range(4):
                split_into(leafblk, leaf_h, leaf_l, n, RANK)
            for copy in points_in:
                copy.wait_recv()
            for w in (0, 1, 4, 5):
                turn(w)
            for l in range(2):
                for j in range(3):
                    tile(l, j, near_place(l, j))
        for copy in chips_in:
            copy.wait_recv()
        hown[p] = sum(product(stacked(gchip[p, i]), chip_h[i], chip_l[i]) for i in range(4))
        h_in = send(hown.at[p], hrecv.at[p], (leaf, other))
        if p == 1:
            squares = start_round(1, sum_round(0, squares))
        for copy in values_in:
            copy.wait_recv()
        for l in range(2):
            near[l] = near[l] + sum(near_term(p, l, j, near_place(l, j)) for j in range(3))
        for copy in coeff_in:
            copy.wait_recv()
        local = [
            sum(
                product(stacked(cwin[p][place(far_ref[l, j])]), leaf_h[2 * l + j], leaf_l[2 * l + j])
                for j in range(2)
            )
            for l in range(2)
        ]
        if p == 1:
            squares = start_round(2, sum_round(1, squares))
        h_in.wait_recv()
        h = stacked(hown[p] + hrecv[p])
        done = []
        for l in range(2):
            e = local[l] + product(h, trans_h[l], trans_l[l], NT)
            done.append(near[l] + product(stacked(e), basis_h[l], basis_l[l], NT))
        if p == 0:
            for l in range(2):
                vwin[1][2 + l] = done[l]
        else:
            second = stacked(jnp.concatenate(done, axis=1))
            placed = lax.dot_general(second, perm[...], NT, preferred_element_type=F32)
            total = sum_round(2, squares)
            scale = lax.rsqrt(total * (1.0 / POINTS) + EPSILON)
            wide = jnp.broadcast_to(scale[0:1, :], (COLS, 128))
            diagonal = lax.broadcasted_iota(jnp.int32, (COLS, 128), 0) == lax.broadcasted_iota(
                jnp.int32, (COLS, 128), 1
            )
            column = jnp.sum(jnp.where(diagonal, wide, 0.0), axis=1, keepdims=True)
            out_ref[...] = (placed[:COLS] + placed[COLS:]) * column
    for copy in sent:
        copy.wait_send()


def on_device(
    probes, points, leaf_order, near_list, far_leaf_list, far_chip_list,
    leaf_basis, transfer, far_leaf_blocks, far_chip_blocks,
):
    smem = pl.BlockSpec(memory_space=pltpu.SMEM)
    anywhere = pl.BlockSpec(memory_space=pl.ANY)
    vmem = pltpu.VMEM
    dma = pltpu.SemaphoreType.DMA
    return pl.pallas_call(
        kernel,
        out_shape=jax.ShapeDtypeStruct((COLS, 1024), F32),
        in_specs=[smem] * 3 + [anywhere] * 7,
        out_specs=pl.BlockSpec(memory_space=pltpu.VMEM),
        scratch_shapes=[
            vmem((COLS, 1024), F32),
            vmem((3, 1024), F32),
            vmem((8, 128), jnp.int32),
            vmem((2, LEAF, RANK), F32),
            vmem((2, RANK, RANK), F32),
            vmem((4, RANK, RANK), F32),
            vmem((8, RANK, RANK), F32),
            vmem((1024, 1024), BF16),
            vmem((2, LEAF, RANK), BF16),
            vmem((2, LEAF, RANK), BF16),
            vmem((2, RANK, RANK), BF16),
            vmem((2, RANK, RANK), BF16),
            vmem((4, RANK, RANK), BF16),
            vmem((4, RANK, RANK), BF16),
            vmem((4, RANK, RANK), BF16),
            vmem((4, RANK, RANK), BF16),
            vmem((8, LEAF, LEAF), BF16),
            vmem((8, LEAF, LEAF), BF16),
            vmem((6, LEAF, 128), F32),
            vmem((6, 8, LEAF), F32),
            vmem((6, COLS, LEAF), F32),
            vmem((6, COLS, LEAF), F32),
            vmem((6, COLS, RANK), F32),
            vmem((6, COLS, RANK), F32),
            vmem((2, COLS, RANK), F32),
            vmem((2, COLS, RANK), F32),
            vmem((2, COLS, RANK), F32),
            vmem((2, 4, COLS, RANK), F32),
            vmem((2, COLS, RANK), F32),
            vmem((2, COLS, RANK), F32),
            vmem((2, COLS, LEAF), F32),
            vmem((3, 8, 128), F32),
            vmem((17, 8, 128), F32),
            dma((7,)),
            dma((39,)),
            dma((39,)),
        ],
        compiler_params=pltpu.CompilerParams(
            collective_id=0, has_side_effects=True, vmem_limit_bytes=56 * 1024 * 1024
        ),
    )(
        near_list, far_leaf_list, far_chip_list, probes, points, leaf_order.reshape(8, 128),
        leaf_basis, transfer, far_leaf_blocks, far_chip_blocks,
    )


def solution(mesh):
    both = ("leaf", "sub")
    return jax.shard_map(
        on_device,
        mesh=mesh,
        in_specs=(
            P(None, both), P(None, both), P(both), P(both, None), P(both, None), P("leaf", None),
            P(both, None, None), P(both, None, None), P(both, None, None), P("leaf", None, None),
        ),
        out_specs=P(None, both),
        check_vma=False,
    )
```

profile of v0, /device:TPU:1, one launch (start us, length us, event | category | flops | bytes accessed | tf_op | source)
XLA Modules:
  0.0 51.3 jit_solution(10289100851181943434)
XLA Ops:
  0.0 49.6 %shard_map.100 = f32[64,1024]{1,0:T(8,128)} custom-call(s32[2,4]{1,0:T(2,128)} %near_ref.1, s32[2,2]{1,0:T(2,128)} %far_ref.1, s32[1,8]{1,0:T(1,128)} %chip_ref.1, f32[64,1024]{1,0:T(8,128)} %probes_hbm.1, f32[3,1024]{1,0:T(4,128)} %points_hbm.1, s32[8,128]{1,0:T(8,128)} %bitcast.1, f32[2,512,256]{2,1,0:T(8,128)} %basis_hbm.1, f32[2,256,256]{2,1,0:T(8,128)} %transfer_hbm.1, ...), custom_call_target="tpu_custom_call" | custom-call | tf_op jit(solution)/shard_map/pallas_call | solution.py:328
  49.6 1.7 %copy.12 = f32[64,1024]{1,0:T(8,128)} copy(f32[64,1024]{1,0:T(8,128)} %shard_map.100) | data formatting | bytes 524288
where the time goes:
time: 51.7 us; the launch traced here: 51.3 us
  Pallas kernels  49.6 us (96%)
  local copies, waits for them, and re-layouts  1.67 us (3%)
    pallas_call x1, Pallas kernels, on_device(): pl.pallas_call(kernel, out_shape=jax.ShapeDtypeStruct((COLS, 1024), F32),...  49.6 us
    unnamed x1, local copies, waits for them, and re-layouts  1.67 us

commit v1 on v0

--- a/solution.py
+++ b/solution.py
@@ -81,9 +81,8 @@
         return (((z + dz) % NZ) * NX + (x + dx) % NX) * NY + (y + dy) % NY
 
     rounds = (
-        [(chip_of(0, 0, dy), (sub + ds) % 2) for dy in range(NY) for ds in range(2) if dy + ds > 0],
-        [(chip_of(0, dx, 0), sub) for dx in range(1, NX)],
-        [(chip_of(dz, 0, 0), sub) for dz in range(1, NZ)],
+        [(chip_of(0, dx, dy), sub) for dx in range(NX) for dy in range(NY) if dx + dy > 0],
+        [(chip_of(dz, 0, 0), (sub + ds) % 2) for dz in range(NZ) for ds in range(2) if dz + ds > 0],
     )
 
     barrier = pltpu.get_barrier_semaphore()
@@ -126,11 +125,11 @@
         sent.append(copy)
         return copy
 
-    def both_ways(ref):
-        return (
-            send(ref.at[pl.ds(2, 2)], ref.at[pl.ds(0, 2)], (nxt, other)),
-            send(ref.at[pl.ds(2, 2)], ref.at[pl.ds(4, 2)], (prv, other)),
-        )
+    def both_ways(ref, at=2, n=2):
+        return [
+            send(ref.at[pl.ds(at, n)], ref.at[pl.ds(at - 2, n)], (nxt, other)),
+            send(ref.at[pl.ds(at, n)], ref.at[pl.ds(at + 2, n)], (prv, other)),
+        ]
 
     points_in = both_ways(pwin)
 
@@ -163,7 +162,7 @@
         tx, ty, tz = target[0:1], target[1:2], target[2:3]
 
         def step(i, _):
-            part = pl.ds(pl.multiple_of(i * 32, 32), 32)
+            part = pl.ds(pl.multiple_of(i * 64, 64), 64)
             s = turned[source, part, :]
             dx = s[:, 0:1] - tx
             dy = s[:, 1:2] - ty
@@ -172,7 +171,7 @@
             kern_h[4 * l + j, part, :] = a
             kern_l[4 * l + j, part, :] = b
             return 0
-        lax.fori_loop(0, LEAF // 32, step, 0)
+        lax.fori_loop(0, LEAF // 64, step, 0, unroll=4)
 
     def turn(w):
         whole = jnp.concatenate([pwin[w], jnp.zeros((120, LEAF), F32)], axis=0)
@@ -182,7 +181,7 @@
         return product(stacked(vwin[p][w]), kern_h[4 * l + j], kern_l[4 * l + j])
 
     def sum_round(r, copies):
-        base = (0, 7, 10)[r]
+        base = 15 * r
         for i, copy in enumerate(copies):
             copy.wait_recv()
         total = sqown[r]
@@ -191,7 +190,7 @@
         return total
 
     def start_round(r, total):
-        base = (0, 7, 10)[r]
+        base = 15 * r
         sqown[r] = total
         return [send(sqown.at[r], sqrecv.at[base + i], who) for i, who in enumerate(rounds[r])]
 
@@ -212,33 +211,37 @@
                 split_into(transfer, trans_h, trans_l, l, RANK)
         gown[p] = sum(product(stacked(up[l]), trans_h[l], trans_l[l]) for l in range(2))
         g_in = send(gown.at[p], grecv.at[p], (leaf, other))
-        values_in = None
-        if p == 0:
-            values_in = both_ways(vwin[p])
+        if p == 0:
             for l in range(2):
                 turn(2 + l)
-        if p == 0:
             for l in range(2):
                 tile(l, 3, 2 + l)
+        else:
+            values_in = ahead + both_ways(vwin[1], 3, 1)
+            total = jnp.zeros((COLS, 128), F32)
+            for l in range(2):
+                v = vwin[1][2 + l]
+                v = v * v
+                for k in range(4):
+                    total = total + v[:, k * 128:(k + 1) * 128]
+            total = lax.dot_general(
+                jnp.ones((8, 128), F32), jnp.concatenate([total, total], axis=0), NT,
+                precision=lax.Precision.HIGHEST, preferred_element_type=F32,
+            )
+            squares = start_round(0, total)
         g_in.wait_recv()
         gsum[p] = gown[p] + grecv[p]
         chips_in = [
             send(gsum.at[p], gchip.at[p, i], ((leaf + sign * d + CHIPS) % CHIPS, sub))
             for i, d in enumerate(DISTANCES)
         ]
-        if values_in is None:
-            values_in = both_ways(vwin[p])
+        if p == 0:
+            values_in = both_ways(vwin[0])
         coeff_in = both_ways(cwin[p])
-        if p == 1:
-            v = jnp.concatenate([vwin[p][2], vwin[p][3]], axis=1)
-            v = v * v
-            total = lax.dot_general(
-                jnp.ones((8, 1024), F32), jnp.concatenate([v, v], axis=0), NT,
-                precision=lax.Precision.HIGHEST, preferred_element_type=F32,
-            )
-            squares = start_round(0, total)
         for l in range(2):
             near[l] = near_term(p, l, 3, 2 + l)
+        if p == 1:
+            squares = start_round(1, sum_round(0, squares))
         if p == 0:
             ld_chip.wait()
             for i, d in enumerate(DISTANCES):
@@ -276,8 +279,6 @@
             copy.wait_recv()
         hown[p] = sum(product(stacked(gchip[p, i]), chip_h[i], chip_l[i]) for i in range(4))
         h_in = send(hown.at[p], hrecv.at[p], (leaf, other))
-        if p == 1:
-            squares = start_round(1, sum_round(0, squares))
         for copy in values_in:
             copy.wait_recv()
         for l in range(2):
@@ -291,21 +292,20 @@
             )
             for l in range(2)
         ]
-        if p == 1:
-            squares = start_round(2, sum_round(1, squares))
         h_in.wait_recv()
         h = stacked(hown[p] + hrecv[p])
         done = []
         for l in range(2):
             e = local[l] + product(h, trans_h[l], trans_l[l], NT)
             done.append(near[l] + product(stacked(e), basis_h[l], basis_l[l], NT))
-        if p == 0:
-            for l in range(2):
+            if p == 0:
                 vwin[1][2 + l] = done[l]
-        else:
+                if l == 0:
+                    ahead = both_ways(vwin[1], 2, 1)
+        if p == 1:
             second = stacked(jnp.concatenate(done, axis=1))
             placed = lax.dot_general(second, perm[...], NT, preferred_element_type=F32)
-            total = sum_round(2, squares)
+            total = sum_round(1, squares)
             scale = lax.rsqrt(total * (1.0 / POINTS) + EPSILON)
             wide = jnp.broadcast_to(scale[0:1, :], (COLS, 128))
             diagonal = lax.broadcasted_iota(jnp.int32, (COLS, 128), 0) == lax.broadcasted_iota(
@@ -362,11 +362,11 @@
             vmem((2, COLS, RANK), F32),
             vmem((2, COLS, RANK), F32),
             vmem((2, COLS, LEAF), F32),
-            vmem((3, 8, 128), F32),
-            vmem((17, 8, 128), F32),
+            vmem((2, 8, 128), F32),
+            vmem((30, 8, 128), F32),
             dma((7,)),
-            dma((39,)),
-            dma((39,)),
+            dma((54,)),
+            dma((54,)),
         ],
         compiler_params=pltpu.CompilerParams(
             collective_id=0, has_side_effects=True, vmem_limit_bytes=56 * 1024 * 1024

time: 51.7 us -> 44.7 us (0.86)
  Pallas kernels: 49.6 us -> 42.3 us
    pallas_call x1, Pallas kernels: 49.6 us -> 42.3 us  [on_device(): pl.pallas_call(kernel, out_shape=jax.ShapeDtypeStruct((COLS, 1024), F32),...]
where the time goes in v1:
time: 44.7 us; the launch traced here: 44 us
  Pallas kernels  42.3 us (95%)
  local copies, waits for them, and re-layouts  1.67 us (4%)
    pallas_call x1, Pallas kernels, on_device(): pl.pallas_call(kernel, out_shape=jax.ShapeDtypeStruct((COLS, 1024), F32),...  42.3 us
    unnamed x1, local copies, waits for them, and re-layouts  1.67 us

profile of v1, /device:TPU:1, one launch (start us, length us, event | category | flops | bytes accessed | tf_op | source)
XLA Modules:
  0.0 44.0 jit_solution(14215900508605051366)
XLA Ops:
  0.0 42.3 %shard_map.100 = f32[64,1024]{1,0:T(8,128)} custom-call(s32[2,4]{1,0:T(2,128)} %near_ref.1, s32[2,2]{1,0:T(2,128)} %far_ref.1, s32[1,8]{1,0:T(1,128)} %chip_ref.1, f32[64,1024]{1,0:T(8,128)} %probes_hbm.1, f32[3,1024]{1,0:T(4,128)} %points_hbm.1, s32[8,128]{1,0:T(8,128)} %bitcast.1, f32[2,512,256]{2,1,0:T(8,128)} %basis_hbm.1, f32[2,256,256]{2,1,0:T(8,128)} %transfer_hbm.1, ...), custom_call_target="tpu_custom_call" | custom-call | tf_op jit(solution)/shard_map/pallas_call | solution.py:328
  42.3 1.7 %copy.12 = f32[64,1024]{1,0:T(8,128)} copy(f32[64,1024]{1,0:T(8,128)} %shard_map.100) | data formatting | bytes 524288

commit v2 on v1

--- a/solution.py
+++ b/solution.py
@@ -21,7 +21,7 @@
 NY = 4
 NX = 4
 NZ = 8
-DISTANCES = (2, 3, 4, 5)
+DISTANCES = (5, 2, 3, 4)
 EXPONENT = -0.5 / (0.15 * 0.15) * math.log2(math.e)
 EPSILON = 1e-6
 NN = (((1,), (0,)), ((), ()))
@@ -64,8 +64,7 @@
     y = leaf % NY
     x = (leaf // NY) % NX
     z = leaf // (NY * NX)
-    nxt = ((dev + 1) % DEVICES) // 2
-    prv = ((dev + DEVICES - 1) % DEVICES) // 2
+    across = (leaf + sign + CHIPS) % CHIPS
 
     loads = []
     for n, (src, dst) in enumerate((
@@ -86,7 +85,7 @@
     )
 
     barrier = pltpu.get_barrier_semaphore()
-    senders = [(nxt, other), (prv, other)]
+    senders = [(across, other), (leaf, other)]
     senders += [((leaf - sign * d + CHIPS) % CHIPS, sub) for d in DISTANCES]
     senders += [who for group in rounds for who in group]
     for who in senders:
@@ -127,8 +126,8 @@
 
     def both_ways(ref, at=2, n=2):
         return [
-            send(ref.at[pl.ds(at, n)], ref.at[pl.ds(at - 2, n)], (nxt, other)),
-            send(ref.at[pl.ds(at, n)], ref.at[pl.ds(at + 2, n)], (prv, other)),
+            send(ref.at[pl.ds(at, n)], ref.at[pl.ds(at + 2 - 4 * sub, n)], (across, other)),
+            send(ref.at[pl.ds(at, n)], ref.at[pl.ds(at - 2 + 4 * sub, n)], (leaf, other)),
         ]
 
     points_in = both_ways(pwin)
@@ -138,6 +137,7 @@
     v_sorted = v_sorted[:COLS] + v_sorted[COLS:]
     for l in range(2):
         vwin[0][2 + l] = v_sorted[:, l * LEAF:(l + 1) * LEAF]
+    values_in = both_ways(vwin[0])
 
     first_leaf = 2 * (dev - 1)
 
@@ -214,10 +214,33 @@
         if p == 0:
             for l in range(2):
                 turn(2 + l)
-            for l in range(2):
-                tile(l, 3, 2 + l)
+            ld_chip.wait()
+            for i, d in enumerate(DISTANCES):
+                want = jnp.where(sub == 0, d, CHIPS - d)
+                slot = jnp.int32(0)
+                found = jnp.int32(0)
+                for j in range(8):
+                    listed = chip_ref[0, j]
+                    hit = jnp.where(
+                        (listed >= 0) & (lax.rem(listed - leaf + CHIPS, CHIPS) == want), 1, 0
+                    )
+                    slot = slot + j * hit
+                    found = found + hit
+                slot = jnp.clip(slot, 0, 7)
+                weight = found.astype(F32)
+
+                def step(k, _, i=i, slot=slot, weight=weight):
+                    part = pl.ds(pl.multiple_of(k * 64, 64), 64)
+                    a, b = parts_of(chipblk[slot, part, :] * weight)
+                    chip_h[i, part, :] = a
+                    chip_l[i, part, :] = b
+                    return 0
+                lax.fori_loop(0, RANK // 64, step, 0)
+            ld_leaf.wait()
+            for n in range(4):
+                split_into(leafblk, leaf_h, leaf_l, n, RANK)
         else:
-            values_in = ahead + both_ways(vwin[1], 3, 1)
+            values_in = ahead
             total = jnp.zeros((COLS, 128), F32)
             for l in range(2):
                 v = vwin[1][2 + l]
@@ -235,39 +258,15 @@
             send(gsum.at[p], gchip.at[p, i], ((leaf + sign * d + CHIPS) % CHIPS, sub))
             for i, d in enumerate(DISTANCES)
         ]
-        if p == 0:
-            values_in = both_ways(vwin[0])
         coeff_in = both_ways(cwin[p])
+        if p == 0:
+            for l in range(2):
+                tile(l, 3, 2 + l)
         for l in range(2):
             near[l] = near_term(p, l, 3, 2 + l)
         if p == 1:
             squares = start_round(1, sum_round(0, squares))
         if p == 0:
-            ld_chip.wait()
-            for i, d in enumerate(DISTANCES):
-                want = jnp.where(sub == 0, d, CHIPS - d)
-                slot = jnp.int32(0)
-                found = jnp.int32(0)
-                for j in range(8):
-                    listed = chip_ref[0, j]
-                    hit = jnp.where(
-                        (listed >= 0) & (lax.rem(listed - leaf + CHIPS, CHIPS) == want), 1, 0
-                    )
-                    slot = slot + j * hit
-                    found = found + hit
-                slot = jnp.clip(slot, 0, 7)
-                weight = found.astype(F32)
-
-                def step(k, _, i=i, slot=slot, weight=weight):
-                    part = pl.ds(pl.multiple_of(k * 64, 64), 64)
-                    a, b = parts_of(chipblk[slot, part, :] * weight)
-                    chip_h[i, part, :] = a
-                    chip_l[i, part, :] = b
-                    return 0
-                lax.fori_loop(0, RANK // 64, step, 0)
-            ld_leaf.wait()
-            for n in range(4):
-                split_into(leafblk, leaf_h, leaf_l, n, RANK)
             for copy in points_in:
                 copy.wait_recv()
             for w in (0, 1, 4, 5):
@@ -300,8 +299,7 @@
             done.append(near[l] + product(stacked(e), basis_h[l], basis_l[l], NT))
             if p == 0:
                 vwin[1][2 + l] = done[l]
-                if l == 0:
-                    ahead = both_ways(vwin[1], 2, 1)
+                ahead = (ahead if l else []) + both_ways(vwin[1], 2 + l, 1)
         if p == 1:
             second = stacked(jnp.concatenate(done, axis=1))
             placed = lax.dot_general(second, perm[...], NT, preferred_element_type=F32)
@@ -327,7 +325,7 @@
     dma = pltpu.SemaphoreType.DMA
     return pl.pallas_call(
         kernel,
-        out_shape=jax.ShapeDtypeStruct((COLS, 1024), F32),
+        out_shape=pltpu.VMEM((COLS, 1024), F32),
         in_specs=[smem] * 3 + [anywhere] * 7,
         out_specs=pl.BlockSpec(memory_space=pltpu.VMEM),
         scratch_shapes=[

time: 44.7 us -> 41.5 us (0.928); the launches traced: 44 us -> 41.4 us
  Pallas kernels: 42.3 us -> 40.6 us
  local copies, waits for them, and re-layouts: 1.67 us -> 0.71 us
    pallas_call x1, Pallas kernels: 42.3 us -> 40.6 us  [on_device(): pl.pallas_call(kernel, out_shape=pltpu.VMEM((COLS, 1024), F32), in_specs=...]
    unnamed x1, local copies, waits for them, and re-layouts: 1.67 us -> 0.71 us
where the time goes in v2:
time: 41.5 us; the launch traced here: 41.4 us
  Pallas kernels  40.6 us (98%)
  local copies, waits for them, and re-layouts  0.71 us (2%)
    pallas_call x1, Pallas kernels, on_device(): pl.pallas_call(kernel, out_shape=pltpu.VMEM((COLS, 1024), F32), in_specs=...  40.6 us

profile of v2, /device:TPU:1, one launch (start us, length us, event | category | flops | bytes accessed | tf_op | source)
XLA Modules:
  0.0 41.4 jit_solution(6818228678858218068)
XLA Ops:
  0.0 40.6 %shard_map.100 = f32[64,1024]{1,0:T(8,128)S(1)} custom-call(s32[2,4]{1,0:T(2,128)} %near_ref.1, s32[2,2]{1,0:T(2,128)} %far_ref.1, s32[1,8]{1,0:T(1,128)} %chip_ref.1, f32[64,1024]{1,0:T(8,128)} %probes_hbm.1, f32[3,1024]{1,0:T(4,128)} %points_hbm.1, s32[8,128]{1,0:T(8,128)} %bitcast.1, f32[2,512,256]{2,1,0:T(8,128)} %basis_hbm.1, ...), custom_call_target="tpu_custom_call" | custom-call | tf_op jit(solution)/shard_map/pallas_call | solution.py:326
  40.6 0.7 %copy.12 = f32[64,1024]{1,0:T(8,128)} copy(f32[64,1024]{1,0:T(8,128)S(1)} %shard_map.100) | data formatting | bytes 524288
